TPU v7x, 256 devices: a whole 4x4x8 slice. The times are simulated.
256 devices in a mesh: seq: 64 (over z, y_lo, x), ch: 4 (over y_hi, core).
Axes of the slice: x: 4, y: 4 (y_hi: 2, y_lo: 2; y = y_hi * 2 + y_lo), z: 8, core: 2. Of those that a mesh axis runs over, the one named last changes fastest.
Arguments:
- query_gate: float32 [16384, 4096], P('seq', 'ch'), may hold values from -6 to 6
- key_gate: float32 [16384, 4096], P('seq', 'ch'), may hold values from -6 to 6
- value_in: float32 [16384, 4096], P('seq', 'ch'), may hold values from -6 to 6
- filters: float32 [2048, 4096], P('seq', 'ch'), may hold values from -2 to 2
- skip_gain: float32 [4096], P('ch'), may hold values from 0.1 to 1.9
Outputs:
- output: float32 [16384, 4096], P('seq', 'ch')
All inputs are finite; a program needn't handle non-finite values.
Results may differ from a plain program's by a relative error of at most 0.0003.
Values sent between devices are 32-bit elements; how exact they have to be, the bound alone decides.
A program may use at most 128 MiB of HBM per device.

v0:
```python
import jax
import jax.numpy as jnp
from jax import lax
from jax.sharding import PartitionSpec as P

ROUNDS = 8


def from_behind(value, axis, by):
    size = lax.axis_size(axis)
    pairs = [(i, i + by) for i in range(size) if 0 <= i + by < size]
    return lax.ppermute(value, axis, pairs)


def tables(block):
    freq = jnp.arange(block, dtype=jnp.int32)
    times = jnp.arange(2 * block, dtype=jnp.int32)
    phase = freq[:, None] * times[None, :] % (2 * block)
    angle = phase.astype(jnp.float32) * (jnp.pi / block)
    signs = 1.0 - 2.0 * (times % 2).astype(jnp.float32)
    late = block + jnp.arange(block, dtype=jnp.int32)
    back_phase = late[:, None] * freq[None, :] % (2 * block)
    back_angle = back_phase.astype(jnp.float32) * (jnp.pi / block)
    weight = jnp.where(freq == 0, 1.0, 2.0).astype(jnp.float32) / (2.0 * block)
    back_signs = (1.0 - 2.0 * (late % 2).astype(jnp.float32)) / (2.0 * block)
    return (
        jnp.cos(angle),
        jnp.sin(angle),
        signs,
        jnp.cos(back_angle) * weight[None, :],
        jnp.sin(back_angle) * weight[None, :],
        back_signs,
    )


def matmul(left, right):
    return jnp.dot(left, right, precision=lax.Precision.HIGHEST, preferred_element_type=jnp.float32)


def on_device(query_gate, key_gate, value_in, filters, skip_gain):
    block = query_gate.shape[0]
    mixed = key_gate * value_in
    cos_tab, sin_tab, signs, back_cos, back_sin, back_signs = tables(block)
    previous = from_behind(mixed, "seq", 1)
    whole = lax.all_gather(filters, "seq", axis=0, tiled=True)
    lag_blocks = whole.reshape(ROUNDS, block, whole.shape[1])
    zeros = jnp.zeros_like(mixed)
    totals = (zeros, zeros, jnp.zeros((mixed.shape[1],), jnp.float32))
    window = jnp.concatenate([previous, mixed], axis=0)
    spec_real = matmul(cos_tab, window)
    spec_imag = -matmul(sin_tab, window)
    spec_nyq = jnp.sum(signs[:, None] * window, axis=0)
    for lag in range(ROUNDS):
        if lag > 0:
            spec_real, spec_imag, spec_nyq = from_behind((spec_real, spec_imag, spec_nyq), "seq", 1)
        segment = lag_blocks[lag]
        filt_real = matmul(cos_tab[:, :block], segment)
        filt_imag = -matmul(sin_tab[:, :block], segment)
        filt_nyq = jnp.sum(signs[:block, None] * segment, axis=0)
        totals = (
            totals[0] + filt_real * spec_real - filt_imag * spec_imag,
            totals[1] + filt_real * spec_imag + filt_imag * spec_real,
            totals[2] + filt_nyq * spec_nyq,
        )
    conv = (
        matmul(back_cos, totals[0])
        - matmul(back_sin, totals[1])
        + back_signs[:, None] * totals[2][None, :]
    )
    return query_gate * (conv + skip_gain[None, :] * mixed)


def solution(mesh):
    in_specs = (P("seq", "ch"), P("seq", "ch"), P("seq", "ch"), P("seq", "ch"), P("ch"))
    out_specs = P("seq", "ch")
    return jax.shard_map(
        on_device, mesh=mesh, in_specs=in_specs, out_specs=out_specs, check_vma=False
    )
```

profile of v0, /device:TPU:128, one launch (start us, length us, event | category | flops | bytes accessed | tf_op | source)
XLA Modules:
  0.0 540.7 jit_solution(14932279812415148789)
XLA Ops:
  9.0 3.4 collective-permute-start
  12.4 34.3 %collective-permute-done = f32[256,1024]{1,0:T(8,128)S(1)} collective-permute-done((f32[256,1024]{1,0:T(8,128)S(1)}, f32[256,1024]{1,0:T(8,128)S(1)}, u32[]{:S(2)}, u32[]{:S(2)}) %collective-permute-start) | collective-permute-done | bytes 1048608 | tf_op jit(solution)/shard_map/ppermute | solution.py:12
  46.7 4.8 fusion.165
  53.4 3.8 fusion.4
  57.3 1.9 collective-permute-start.1
  59.2 33.9 %collective-permute-done.2 = f32[256,1024]{1,0:T(8,128)S(1)} collective-permute-done((f32[256,1024]{1,0:T(8,128)S(1)}, f32[256,1024]{1,0:T(8,128)S(1)}, u32[]{:S(2)}, u32[]{:S(2)}) %collective-permute-start.2) | collective-permute-done | bytes 1048608 | tf_op jit(solution)/shard_map/ppermute | solution.py:12
  96.0 29.6 %collective-permute-done.1 = f32[256,1024]{1,0:T(8,128)S(1)} collective-permute-done((f32[256,1024]{1,0:T(8,128)S(1)}, f32[256,1024]{1,0:T(8,128)S(1)}, u32[]{:S(2)}, u32[]{:S(2)}) %collective-permute-start.1) | collective-permute-done | bytes 1048608 | tf_op jit(solution)/shard_map/ppermute | solution.py:12
  127.6 30.8 %collective-permute-done.4 = f32[256,1024]{1,0:T(8,128)S(1)} collective-permute-done((f32[256,1024]{1,0:T(8,128)S(1)}, f32[256,1024]{1,0:T(8,128)S(1)}, u32[]{:S(2)}, u32[]{:S(2)}) %collective-permute-start.4) | collective-permute-done | bytes 1048608 | tf_op jit(solution)/shard_map/ppermute | solution.py:12
  160.3 30.6 %collective-permute-done.3 = f32[256,1024]{1,0:T(8,128)S(1)} collective-permute-done((f32[256,1024]{1,0:T(8,128)S(1)}, f32[256,1024]{1,0:T(8,128)S(1)}, u32[]{:S(2)}, u32[]{:S(2)}) %collective-permute-start.3) | collective-permute-done | bytes 1048608 | tf_op jit(solution)/shard_map/ppermute | solution.py:12
  192.9 30.8 %collective-permute-done.6 = f32[256,1024]{1,0:T(8,128)S(1)} collective-permute-done((f32[256,1024]{1,0:T(8,128)S(1)}, f32[256,1024]{1,0:T(8,128)S(1)}, u32[]{:S(2)}, u32[]{:S(2)}) %collective-permute-start.6) | collective-permute-done | bytes 1048608 | tf_op jit(solution)/shard_map/ppermute | solution.py:12
  225.6 30.6 %collective-permute-done.5 = f32[256,1024]{1,0:T(8,128)S(1)} collective-permute-done((f32[256,1024]{1,0:T(8,128)S(1)}, f32[256,1024]{1,0:T(8,128)S(1)}, u32[]{:S(2)}, u32[]{:S(2)}) %collective-permute-start.5) | collective-permute-done | bytes 1048608 | tf_op jit(solution)/shard_map/ppermute | solution.py:12
  258.2 30.8 %collective-permute-done.8 = f32[256,1024]{1,0:T(8,128)S(1)} collective-permute-done((f32[256,1024]{1,0:T(8,128)S(1)}, f32[256,1024]{1,0:T(8,128)S(1)}, u32[]{:S(2)}, u32[]{:S(2)}) %collective-permute-start.8) | collective-permute-done | bytes 1048608 | tf_op jit(solution)/shard_map/ppermute | solution.py:12
  290.9 25.4 %collective-permute-done.7 = f32[256,1024]{1,0:T(8,128)S(1)} collective-permute-done((f32[256,1024]{1,0:T(8,128)S(1)}, f32[256,1024]{1,0:T(8,128)S(1)}, u32[]{:S(2)}, u32[]{:S(2)}) %collective-permute-start.7) | collective-permute-done | bytes 1048608 | tf_op jit(solution)/shard_map/ppermute | solution.py:12
  318.2 22.0 %collective-permute-done.10 = f32[256,1024]{1,0:T(8,128)S(1)} collective-permute-done((f32[256,1024]{1,0:T(8,128)S(1)}, f32[256,1024]{1,0:T(8,128)S(1)}, u32[]{:S(2)}, u32[]{:S(2)}) %collective-permute-start.10) | collective-permute-done | bytes 1048608 | tf_op jit(solution)/shard_map/ppermute | solution.py:12
  342.1 20.5 %collective-permute-done.9 = f32[256,1024]{1,0:T(8,128)S(1)} collective-permute-done((f32[256,1024]{1,0:T(8,128)S(1)}, f32[256,1024]{1,0:T(8,128)S(1)}, u32[]{:S(2)}, u32[]{:S(2)}) %collective-permute-start.9) | collective-permute-done | bytes 1048608 | tf_op jit(solution)/shard_map/ppermute | solution.py:12
  364.8 1.9 collective-permute-start.15
  366.7 39.4 %collective-permute-done.15 = f32[1024]{0:T(1024)S(1)} collective-permute-done((f32[1024]{0:T(1024)S(1)}, f32[1024]{0:T(1024)S(1)}, u32[]{:S(2)}, u32[]{:S(2)}) %collective-permute-start.15) | collective-permute-done | bytes 4128 | tf_op jit(solution)/shard_map/ppermute | solution.py:12
  408.1 7.8 %collective-permute-done.16 = f32[1024]{0:T(1024)S(1)} collective-permute-done((f32[1024]{0:T(1024)S(1)}, f32[1024]{0:T(1024)S(1)}, u32[]{:S(2)}, u32[]{:S(2)}) %collective-permute-start.16) | collective-permute-done | bytes 4128 | tf_op jit(solution)/shard_map/ppermute | solution.py:12
  415.9 13.4 %collective-permute-start.17 = (f32[1024]{0:T(1024)S(1)}, f32[1024]{0:T(1024)S(1)}, u32[]{:S(2)}, u32[]{:S(2)}) collective-permute-start(f32[1024]{0:T(1024)S(1)} %collective-permute-done.16), channel_id=1, source_target_pairs={{0,4},{4,8},{8,12},{12,16},{16,20},{20,24},{24,28},{28,32},{32,36}... | collective-permute-start | bytes 12296 | tf_op jit(solution)/shard_map/ppermute | solution.py:12
  435.1 5.9 %collective-permute-done.18 = f32[1024]{0:T(1024)S(1)} collective-permute-done((f32[1024]{0:T(1024)S(1)}, f32[1024]{0:T(1024)S(1)}, u32[]{:S(2)}, u32[]{:S(2)}) %collective-permute-start.18) | collective-permute-done | bytes 4128 | tf_op jit(solution)/shard_map/ppermute | solution.py:12
  442.9 7.8 %collective-permute-done.19 = f32[1024]{0:T(1024)S(1)} collective-permute-done((f32[1024]{0:T(1024)S(1)}, f32[1024]{0:T(1024)S(1)}, u32[]{:S(2)}, u32[]{:S(2)}) %collective-permute-start.19) | collective-permute-done | bytes 4128 | tf_op jit(solution)/shard_map/ppermute | solution.py:12
  452.6 7.8 %collective-permute-done.20 = f32[1024]{0:T(1024)S(1)} collective-permute-done((f32[1024]{0:T(1024)S(1)}, f32[1024]{0:T(1024)S(1)}, u32[]{:S(2)}, u32[]{:S(2)}) %collective-permute-start.20) | collective-permute-done | bytes 4128 | tf_op jit(solution)/shard_map/ppermute | solution.py:12
  462.3 1.9 collective-permute-start.14
  464.3 1.9 collective-permute-start.13
  466.2 2.4 convolution_negate_fusion.6
  468.6 2.5 convolution_negate_fusion.5
  471.2 2.3 convolution_negate_fusion.4
  473.4 2.3 convolution_negate_fusion.3
  489.7 5.2 collective-permute-done.14
  494.8 15.5 %collective-permute-done.13 = f32[256,1024]{1,0:T(8,128)} collective-permute-done((f32[256,1024]{1,0:T(8,128)}, f32[256,1024]{1,0:T(8,128)}, u32[]{:S(2)}, u32[]{:S(2)}) %collective-permute-start.13) | collective-permute-done | bytes 1048608 | tf_op jit(solution)/shard_map/ppermute | solution.py:12
  510.3 11.0 %fusion.5 = f32[256,1024]{1,0:T(8,128)} fusion(f32[256,1024]{1,0:T(8,128)S(1)} %convolution_negate_fusion, f32[256,1024]{1,0:T(8,128)} %collective-permute-done.13, f32[256,1024]{1,0:T(8,128)S(1)} %fusion.70, f32[256,1024]{1,0:T(8,128)} %collective-permute-done.14, f32[256,1024]{1,0:T(8,128)S(1)} %convolution_negate_fusion.1, ...), kind=kOutput, calls=%fused_computation.23 | convolution fusion | flops 814940160 | bytes 34605056 | tf_op jit(solution)/shard_map/dot_general | solution.py:37
  521.4 12.2 %fusion.2 = f32[256,1024]{1,0:T(8,128)} fusion(f32[256,1024]{1,0:T(8,128)} %param.5, f32[256,1024]{1,0:T(8,128)} %fusion.5, f32[256,1024]{1,0:T(8,128)S(1)} %mul.463, f32[256,1024]{1,0:T(8,128)S(1)} %convolution_negate_fusion, f32[256,1024]{1,0:T(8,128)} %collective-permute-done.14, f32[256,1024]{1,0:T(8,128)} %copy-done.1, ...), kind=kOutput, calls=%fused_computation.12 | convolution fusion | flops 815988736 | bytes 37760000 | tf_op jit(solution)/shard_map/dot_general | solution.py:37
  (82 shorter events, 51.9 us)
Async XLA Ops:
  6.5 459.7 %all-gather.2.cloned.1.call-start = ((), (), s32[]{:S(2)}) async-start(), calls=%async_computation | async-start | bytes 8519680 | tf_op jit(solution)/shard_map/all_gather | solution.py:45
  9.0 37.7 %collective-permute-start = (f32[256,1024]{1,0:T(8,128)S(1)}, f32[256,1024]{1,0:T(8,128)S(1)}, u32[]{:S(2)}, u32[]{:S(2)}) collective-permute-start(f32[256,1024]{1,0:T(8,128)S(1)} %mul.463), channel_id=1, source_target_pairs={{0,4},{4,8},{8,12},{12,16},{16,20},{20,24},{24,28},{28,32},{32,36}... | collective-permute-start | bytes 3145736 | tf_op jit(solution)/shard_map/ppermute | solution.py:12
  51.5 41.6 %collective-permute-start.2 = (f32[256,1024]{1,0:T(8,128)S(1)}, f32[256,1024]{1,0:T(8,128)S(1)}, u32[]{:S(2)}, u32[]{:S(2)}) collective-permute-start(f32[256,1024]{1,0:T(8,128)S(1)} %get-tuple-element.13), channel_id=1, source_target_pairs={{0,4},{4,8},{8,12},{12,16},{16,20},{20,24},{24,28},{28,32},{32,36}... | collective-permute-start | bytes 3145736 | tf_op jit(solution)/shard_map/ppermute | solution.py:12
  57.3 101.2 %copy-start.6 = (f32[256,1024]{1,0:T(8,128)}, f32[256,1024]{1,0:T(8,128)S(1)}, u32[]{:S(2)}) copy-start(f32[256,1024]{1,0:T(8,128)S(1)} %fusion.4) | copy-start | bytes 3145732
  57.3 68.4 %collective-permute-start.1 = (f32[256,1024]{1,0:T(8,128)S(1)}, f32[256,1024]{1,0:T(8,128)S(1)}, u32[]{:S(2)}, u32[]{:S(2)}) collective-permute-start(f32[256,1024]{1,0:T(8,128)S(1)} %fusion.4), channel_id=1, source_target_pairs={{0,4},{4,8},{8,12},{12,16},{16,20},{20,24},{24,28},{28,32},{32,36}... | collective-permute-start | bytes 3145736 | tf_op jit(solution)/shard_map/ppermute | solution.py:12
  94.1 64.3 %collective-permute-start.4 = (f32[256,1024]{1,0:T(8,128)S(1)}, f32[256,1024]{1,0:T(8,128)S(1)}, u32[]{:S(2)}, u32[]{:S(2)}) collective-permute-start(f32[256,1024]{1,0:T(8,128)S(1)} %collective-permute-done.2), channel_id=1, source_target_pairs={{0,4},{4,8},{8,12},{12,16},{16,20},{20,24},{24,28},{28,32},{32,36}... | collective-permute-start | bytes 3145736 | tf_op jit(solution)/shard_map/ppermute | solution.py:12
  125.7 34.7 %copy-start.7 = (f32[256,1024]{1,0:T(8,128)}, f32[256,1024]{1,0:T(8,128)S(1)}, u32[]{:S(2)}) copy-start(f32[256,1024]{1,0:T(8,128)S(1)} %collective-permute-done.1) | copy-start | bytes 3145732
  125.7 65.3 %collective-permute-start.3 = (f32[256,1024]{1,0:T(8,128)S(1)}, f32[256,1024]{1,0:T(8,128)S(1)}, u32[]{:S(2)}, u32[]{:S(2)}) collective-permute-start(f32[256,1024]{1,0:T(8,128)S(1)} %collective-permute-done.1), channel_id=1, source_target_pairs={{0,4},{4,8},{8,12},{12,16},{16,20},{20,24},{24,28},{28,32},{32,36}... | collective-permute-start | bytes 3145736 | tf_op jit(solution)/shard_map/ppermute | solution.py:12
  158.4 32.6 %copy-start.8 = (f32[256,1024]{1,0:T(8,128)}, f32[256,1024]{1,0:T(8,128)S(1)}, u32[]{:S(2)}) copy-start(f32[256,1024]{1,0:T(8,128)S(1)} %collective-permute-done.4) | copy-start | bytes 3145732
  158.4 65.3 %collective-permute-start.6 = (f32[256,1024]{1,0:T(8,128)S(1)}, f32[256,1024]{1,0:T(8,128)S(1)}, u32[]{:S(2)}, u32[]{:S(2)}) collective-permute-start(f32[256,1024]{1,0:T(8,128)S(1)} %collective-permute-done.4), channel_id=1, source_target_pairs={{0,4},{4,8},{8,12},{12,16},{16,20},{20,24},{24,28},{28,32},{32,36}... | collective-permute-start | bytes 3145736 | tf_op jit(solution)/shard_map/ppermute | solution.py:12
  191.0 32.8 %copy-start.9 = (f32[256,1024]{1,0:T(8,128)}, f32[256,1024]{1,0:T(8,128)S(1)}, u32[]{:S(2)}) copy-start(f32[256,1024]{1,0:T(8,128)S(1)} %collective-permute-done.3) | copy-start | bytes 3145732
  191.0 65.3 %collective-permute-start.5 = (f32[256,1024]{1,0:T(8,128)S(1)}, f32[256,1024]{1,0:T(8,128)S(1)}, u32[]{:S(2)}, u32[]{:S(2)}) collective-permute-start(f32[256,1024]{1,0:T(8,128)S(1)} %collective-permute-done.3), channel_id=1, source_target_pairs={{0,4},{4,8},{8,12},{12,16},{16,20},{20,24},{24,28},{28,32},{32,36}... | collective-permute-start | bytes 3145736 | tf_op jit(solution)/shard_map/ppermute | solution.py:12
  223.7 65.2 %collective-permute-start.8 = (f32[256,1024]{1,0:T(8,128)S(1)}, f32[256,1024]{1,0:T(8,128)S(1)}, u32[]{:S(2)}, u32[]{:S(2)}) collective-permute-start(f32[256,1024]{1,0:T(8,128)S(1)} %collective-permute-done.6), channel_id=1, source_target_pairs={{0,4},{4,8},{8,12},{12,16},{16,20},{20,24},{24,28},{28,32},{32,36}... | collective-permute-start | bytes 3145736 | tf_op jit(solution)/shard_map/ppermute | solution.py:12
  256.3 32.7 %copy-start.11 = (f32[256,1024]{1,0:T(8,128)}, f32[256,1024]{1,0:T(8,128)S(1)}, u32[]{:S(2)}) copy-start(f32[256,1024]{1,0:T(8,128)S(1)} %collective-permute-done.5) | copy-start | bytes 3145732
  256.3 60.0 %collective-permute-start.7 = (f32[256,1024]{1,0:T(8,128)S(1)}, f32[256,1024]{1,0:T(8,128)S(1)}, u32[]{:S(2)}, u32[]{:S(2)}) collective-permute-start(f32[256,1024]{1,0:T(8,128)S(1)} %collective-permute-done.5), channel_id=1, source_target_pairs={{0,4},{4,8},{8,12},{12,16},{16,20},{20,24},{24,28},{28,32},{32,36}... | collective-permute-start | bytes 3145736 | tf_op jit(solution)/shard_map/ppermute | solution.py:12
  289.0 51.2 %collective-permute-start.10 = (f32[256,1024]{1,0:T(8,128)S(1)}, f32[256,1024]{1,0:T(8,128)S(1)}, u32[]{:S(2)}, u32[]{:S(2)}) collective-permute-start(f32[256,1024]{1,0:T(8,128)S(1)} %collective-permute-done.8), channel_id=1, source_target_pairs={{0,4},{4,8},{8,12},{12,16},{16,20},{20,24},{24,28},{28,32},{32,36}... | collective-permute-start | bytes 3145736 | tf_op jit(solution)/shard_map/ppermute | solution.py:12
  316.3 46.3 %collective-permute-start.9 = (f32[256,1024]{1,0:T(8,128)S(1)}, f32[256,1024]{1,0:T(8,128)S(1)}, u32[]{:S(2)}, u32[]{:S(2)}) collective-permute-start(f32[256,1024]{1,0:T(8,128)S(1)} %collective-permute-done.7), channel_id=1, source_target_pairs={{0,4},{4,8},{8,12},{12,16},{16,20},{20,24},{24,28},{28,32},{32,36}... | collective-permute-start | bytes 3145736 | tf_op jit(solution)/shard_map/ppermute | solution.py:12
  340.2 91.1 %copy-start.14 = (f32[256,1024]{1,0:T(8,128)}, f32[256,1024]{1,0:T(8,128)S(1)}, u32[]{:S(2)}) copy-start(f32[256,1024]{1,0:T(8,128)S(1)} %collective-permute-done.10) | copy-start | bytes 3145732
  340.2 122.1 %collective-permute-start.12 = (f32[256,1024]{1,0:T(8,128)S(1)}, f32[256,1024]{1,0:T(8,128)}, u32[]{:S(2)}, u32[]{:S(2)}) collective-permute-start(f32[256,1024]{1,0:T(8,128)S(1)} %collective-permute-done.10), channel_id=1, source_target_pairs={{0,4},{4,8},{8,12},{12,16},{16,20},{20,24},{24,28},{28,32},{32,36}... | collective-permute-start | bytes 3145736 | tf_op jit(solution)/shard_map/ppermute | solution.py:12
  362.7 99.7 %copy-start.15 = (f32[256,1024]{1,0:T(8,128)}, f32[256,1024]{1,0:T(8,128)S(1)}, u32[]{:S(2)}) copy-start(f32[256,1024]{1,0:T(8,128)S(1)} %collective-permute-done.9) | copy-start | bytes 3145732
  362.7 101.6 %collective-permute-start.11 = (f32[256,1024]{1,0:T(8,128)S(1)}, f32[256,1024]{1,0:T(8,128)}, u32[]{:S(2)}, u32[]{:S(2)}) collective-permute-start(f32[256,1024]{1,0:T(8,128)S(1)} %collective-permute-done.9), channel_id=1, source_target_pairs={{0,4},{4,8},{8,12},{12,16},{16,20},{20,24},{24,28},{28,32},{32,36}... | collective-permute-start | bytes 3145736 | tf_op jit(solution)/shard_map/ppermute | solution.py:12
  364.6 113.2 %copy-start.16 = (f32[512]{0:T(512)}, f32[512]{0:T(512)S(1)}, u32[]{:S(2)}) copy-start(f32[512]{0:T(512)S(1)} %fusion.136) | copy-start | bytes 6148
  364.8 41.4 %collective-permute-start.15 = (f32[1024]{0:T(1024)S(1)}, f32[1024]{0:T(1024)S(1)}, u32[]{:S(2)}, u32[]{:S(2)}) collective-permute-start(f32[1024]{0:T(1024)S(1)} %multiply_reduce_fusion), channel_id=1, source_target_pairs={{0,4},{4,8},{8,12},{12,16},{16,20},{20,24},{24,28},{28,32},{32,36}... | collective-permute-start | bytes 12296 | tf_op jit(solution)/shard_map/ppermute | solution.py:12
  406.2 9.7 %collective-permute-start.16 = (f32[1024]{0:T(1024)S(1)}, f32[1024]{0:T(1024)S(1)}, u32[]{:S(2)}, u32[]{:S(2)}) collective-permute-start(f32[1024]{0:T(1024)S(1)} %collective-permute-done.15), channel_id=1, source_target_pairs={{0,4},{4,8},{8,12},{12,16},{16,20},{20,24},{24,28},{28,32},{32,36}... | collective-permute-start | bytes 12296 | tf_op jit(solution)/shard_map/ppermute | solution.py:12
  415.9 15.3 %collective-permute-start.17 = (f32[1024]{0:T(1024)S(1)}, f32[1024]{0:T(1024)S(1)}, u32[]{:S(2)}, u32[]{:S(2)}) collective-permute-start(f32[1024]{0:T(1024)S(1)} %collective-permute-done.16), channel_id=1, source_target_pairs={{0,4},{4,8},{8,12},{12,16},{16,20},{20,24},{24,28},{28,32},{32,36}... | collective-permute-start | bytes 12296 | tf_op jit(solution)/shard_map/ppermute | solution.py:12
  431.2 9.7 %collective-permute-start.18 = (f32[1024]{0:T(1024)S(1)}, f32[1024]{0:T(1024)S(1)}, u32[]{:S(2)}, u32[]{:S(2)}) collective-permute-start(f32[1024]{0:T(1024)S(1)} %collective-permute-done.17), channel_id=1, source_target_pairs={{0,4},{4,8},{8,12},{12,16},{16,20},{20,24},{24,28},{28,32},{32,36}... | collective-permute-start | bytes 12296 | tf_op jit(solution)/shard_map/ppermute | solution.py:12
  441.0 9.7 %collective-permute-start.19 = (f32[1024]{0:T(1024)S(1)}, f32[1024]{0:T(1024)S(1)}, u32[]{:S(2)}, u32[]{:S(2)}) collective-permute-start(f32[1024]{0:T(1024)S(1)} %collective-permute-done.18), channel_id=1, source_target_pairs={{0,4},{4,8},{8,12},{12,16},{16,20},{20,24},{24,28},{28,32},{32,36}... | collective-permute-start | bytes 12296 | tf_op jit(solution)/shard_map/ppermute | solution.py:12
  450.7 9.7 %collective-permute-start.20 = (f32[1024]{0:T(1024)S(1)}, f32[1024]{0:T(1024)S(1)}, u32[]{:S(2)}, u32[]{:S(2)}) collective-permute-start(f32[1024]{0:T(1024)S(1)} %collective-permute-done.19), channel_id=1, source_target_pairs={{0,4},{4,8},{8,12},{12,16},{16,20},{20,24},{24,28},{28,32},{32,36}... | collective-permute-start | bytes 12296 | tf_op jit(solution)/shard_map/ppermute | solution.py:12
  460.4 26.1 %collective-permute-start.21 = (f32[1024]{0:T(1024)S(1)}, f32[1024]{0:T(1024)S(1)}, u32[]{:S(2)}, u32[]{:S(2)}) collective-permute-start(f32[1024]{0:T(1024)S(1)} %collective-permute-done.20), channel_id=1, source_target_pairs={{0,4},{4,8},{8,12},{12,16},{16,20},{20,24},{24,28},{28,32},{32,36}... | collective-permute-start | bytes 12296 | tf_op jit(solution)/shard_map/ppermute | solution.py:12
  462.3 32.5 %collective-permute-start.14 = (f32[256,1024]{1,0:T(8,128)}, f32[256,1024]{1,0:T(8,128)}, u32[]{:S(2)}, u32[]{:S(2)}) collective-permute-start(f32[256,1024]{1,0:T(8,128)} %collective-permute-done.12), channel_id=1, source_target_pairs={{0,4},{4,8},{8,12},{12,16},{16,20},{20,24},{24,28},{28,32},{32,36}... | collective-permute-start | bytes 3145736 | tf_op jit(solution)/shard_map/ppermute | solution.py:12
  464.3 46.1 %collective-permute-start.13 = (f32[256,1024]{1,0:T(8,128)}, f32[256,1024]{1,0:T(8,128)}, u32[]{:S(2)}, u32[]{:S(2)}) collective-permute-start(f32[256,1024]{1,0:T(8,128)} %collective-permute-done.11), channel_id=1, source_target_pairs={{0,4},{4,8},{8,12},{12,16},{16,20},{20,24},{24,28},{28,32},{32,36}... | collective-permute-start | bytes 3145736 | tf_op jit(solution)/shard_map/ppermute | solution.py:12
  488.6 32.7 %copy-start.1 = (f32[256,1024]{1,0:T(8,128)}, f32[256,1024]{1,0:T(8,128)S(1)}, u32[]{:S(2)}) copy-start(f32[256,1024]{1,0:T(8,128)S(1)} %fusion.70) | copy-start | bytes 3145732
  (10 other events, 179.4 us)
Sparse Core Ops, SparseCore 0:
  9.1 318.8 all-gather.1
where the time goes:
time: 549 us; the launch traced here: 541 us
  waiting for transfers between devices  409 us (74%)
  starting transfers between devices  55.1 us (10%)
  matrix products  53.7 us (10%)
  between operations  14.3 us (3%)
  other arithmetic  7.13 us (1%)
    ppermute x22, waiting for transfers between devices, from_behind(): return lax.ppermute(value, axis, pairs)  409 us
    ppermute x22, starting transfers between devices, from_behind(): return lax.ppermute(value, axis, pairs)  55.1 us
    dot_general x20, matrix products, matmul(): jnp.dot(left, right, precision=lax.Precision.HIGHEST, preferred_element_t...  53.7 us
  transfers between devices with their start and end apart: 23, of which 18 were waited for; matrix products, arithmetic and copies ran while one was open for 7% of the time, Pallas kernels for 0%

commit v1 on v0

v1 whole, which is shorter than its diff:
```python
import functools

import jax
import jax.numpy as jnp
import numpy as np
from jax import lax
from jax.experimental import pallas as pl
from jax.experimental.pallas import tpu as pltpu
from jax.sharding import PartitionSpec as P

MESH = pl.DeviceIdType.MESH
F32 = jnp.float32
BF16 = jnp.bfloat16
ROWS = 256
LANES = 128
NX, NY, NZ = 4, 2, 8
GROUP = NX * NY
LAGS = ROWS // GROUP
SPEC = 2 * ROWS
PIECES = 2
OFFSETS = [(0, 1), (0, 3), (1, 0), (1, 1), (1, 3), (0, 2), (1, 2)]


def tables():
    m = np.arange(ROWS)
    t = np.arange(ROWS)
    angle = np.pi * (((4 * m[:, None] + 1) * t[None, :]) % (4 * ROWS)) / (2 * ROWS)
    forward = np.concatenate([np.cos(angle), -np.sin(angle)], axis=0)
    back = np.concatenate([-np.sin(angle.T), -np.cos(angle.T)], axis=1) / ROWS
    split = []
    for table in (forward, back):
        high = table.astype(np.float32).astype(jnp.bfloat16)
        low = (table - high.astype(np.float64)).astype(np.float32).astype(jnp.bfloat16)
        split += [high, low]
    return split


def split(value):
    high = value.astype(BF16)
    low = (value - high.astype(F32)).astype(BF16)
    return high, low


def multiply(high_ref, low_ref, value):
    high, low = split(value)
    first = jnp.dot(high_ref[...], jnp.concatenate([high, low], axis=1), preferred_element_type=F32)
    second = jnp.dot(low_ref[...], high, preferred_element_type=F32)
    return first[:, :LANES] + first[:, LANES:] + second


def kernel(
    k_in, v_in, q_in, f_in, s_in, ch_in, cl_in, gh_in, gl_in, out_ref,
    k, v, q, f, s, ch, cl, gh, gl, mix, x, fb, y, fy, w, acc, send, got, out,
    load_sem, fs_sem, fr_sem, ms_sem, mr_sem, hs_sem, hr_sem, rs_sem, rr_sem, os_sem, or_sem, st_sem,
):
    seq = lax.axis_index("seq")
    z, d = seq // GROUP, seq % GROUP
    yy, xx = d // NX, d % NX
    above = ((z + 1) % NZ) * GROUP + d
    below = ((z + NZ - 1) % NZ) * GROUP + d

    def to(o):
        return ((yy + o[0]) % NY) * NX + (xx + o[1]) % NX

    def source(o):
        return ((yy + NY - o[0]) % NY) * NX + (xx + NX - o[1]) % NX

    def remote(src, dst, send_sem, recv_sem, dev):
        return pltpu.make_async_remote_copy(
            src_ref=src, dst_ref=dst, send_sem=send_sem, recv_sem=recv_sem,
            device_id={"seq": dev}, device_id_type=MESH,
        )

    def columns(p):
        return pl.ds(pl.multiple_of(p * LANES, LANES), LANES)

    loads = []
    for i, (a, b) in enumerate(
        [(f_in, f), (k_in, k), (v_in, v), (ch_in, ch), (cl_in, cl), (gh_in, gh), (gl_in, gl), (q_in, q), (s_in, s)]
    ):
        c = pltpu.make_async_copy(a, b, load_sem.at[i])
        c.start()
        loads.append(c)

    barrier = pltpu.get_barrier_semaphore()
    for o in OFFSETS:
        pl.semaphore_signal(barrier, inc=1, device_id={"seq": z * GROUP + to(o)}, device_id_type=MESH)
    for dev in (above, below):
        pl.semaphore_signal(barrier, inc=1, device_id={"seq": dev}, device_id_type=MESH)

    loads[0].wait()
    fb[z, pl.ds(pl.multiple_of(d * LAGS, LAGS), LAGS), :] = f[:, columns(d)]
    loads[1].wait()
    loads[2].wait()
    for p in range(GROUP):
        cols = slice(p * LANES, (p + 1) * LANES)
        mix[p] = k[:, cols] * v[:, cols]
    x[GROUP + d] = mix[d]
    pl.semaphore_wait(barrier, GROUP + 1)

    f_copies, m_copies = [], []
    for n, o in enumerate(OFFSETS):
        p = to(o)
        c = remote(
            f.at[:, columns(p)], fb.at[z, pl.ds(pl.multiple_of(d * LAGS, LAGS), LAGS)],
            fs_sem.at[n], fr_sem.at[n], z * GROUP + p,
        )
        c.start()
        f_copies.append(c)
    h_copies = []

    def halo(n, j):
        c = remote(x.at[GROUP + j], x.at[j], hs_sem.at[n], hr_sem.at[n], above)
        c.start()
        h_copies.append(c)

    halo(GROUP - 1, d)
    for n, o in enumerate(OFFSETS):
        p = to(o)
        c = remote(mix.at[p], x.at[GROUP + d], ms_sem.at[n], mr_sem.at[n], z * GROUP + p)
        c.start()
        m_copies.append(c)

    part = ROWS // PIECES
    r_copies = {}

    def hop(h, i):
        at = pl.ds(i * part, part)
        block = (z + h) % NZ
        c = remote(
            fb.at[block, at], fb.at[block, at], rs_sem.at[h * PIECES + i], rr_sem.at[h * PIECES + i], below
        )
        c.start()
        r_copies[h, i] = c

    def relay(h):
        for i in range(PIECES):
            r_copies[h, i].wait_recv()
            if h + 1 < NZ - 1:
                hop(h + 1, i)

    def arrive(n):
        m_copies[n].wait_recv()
        halo(n, source(OFFSETS[n]))

    def forward(src, block, dst, at):
        dst[at] = multiply(ch, cl, src[block])

    for c in f_copies:
        c.wait_recv()
    for i in range(PIECES):
        hop(0, i)
    for c in loads[3:]:
        c.wait()

    own = GROUP + d
    forward(x, own, y, own)
    forward(fb, z, fy, z)
    for h, group in enumerate([(0, 1), (2, 3), (4, 5), (6,)]):
        for n in group:
            arrive(n)
            j = GROUP + source(OFFSETS[n])
            forward(x, j, y, j)
        relay(h)
        block = (z + h + 1) % NZ
        forward(fb, block, fy, block)

    inside = (z > 0).astype(F32)

    def take(n, j):
        h_copies_by_slot[n].wait_recv()
        y[j] = multiply(ch, cl, x[j] * inside)

    h_copies_by_slot = {}
    for n, c in zip([GROUP - 1] + list(range(GROUP - 1)), h_copies):
        h_copies_by_slot[n] = c

    take(GROUP - 1, d)
    take(0, source(OFFSETS[0]))
    for h in range(4, NZ - 1):
        relay(h)
        block = (z + h + 1) % NZ
        forward(fb, block, fy, block)
        n = h - 3
        take(n, source(OFFSETS[n]))
    for n in range(4, GROUP - 1):
        take(n, source(OFFSETS[n]))

    def window(n, carry):
        def tile(r, carry):
            at = pl.ds(pl.multiple_of(r * 16, 16), 16)
            im = pl.ds(pl.multiple_of(r * 16 + ROWS, 16), 16)
            w[n, at] = y[n, at] + y[n + 1, im]
            w[n, im] = y[n, im] - y[n + 1, at]
            return carry

        return lax.fori_loop(0, ROWS // 16, tile, carry)

    lax.fori_loop(0, 2 * GROUP - 1, window, 0)

    def output(i):
        def tile(r, carry):
            at = pl.ds(pl.multiple_of(r * 8, 8), 8)
            im = pl.ds(pl.multiple_of(r * 8 + ROWS, 8), 8)
            real = jnp.zeros((8, LANES), F32)
            imag = jnp.zeros((8, LANES), F32)
            for j in range(GROUP):
                n = i + GROUP - 1 - j
                fr, fi = fy[j, at], fy[j, im]
                wr, wi = w[n, at], w[n, im]
                real += fr * wr - fi * wi
                imag += fr * wi + fi * wr
            acc[at] = real
            acc[im] = imag
            return carry

        lax.fori_loop(0, ROWS // 8, tile, 0, unroll=2)
        return multiply(gh, gl, acc[...])

    o_copies = []
    for n, o in enumerate(OFFSETS):
        p = to(o)
        send[n] = output(p)
        c = remote(send.at[n], got.at[d], os_sem.at[n], or_sem.at[n], z * GROUP + p)
        c.start()
        o_copies.append(c)
    got[d] = output(d)

    stores = []

    def finish(n, p):
        cols = columns(p)
        out[:, cols] = q[:, cols] * (got[p] + s[:, cols] * mix[p])
        c = pltpu.make_async_copy(out.at[:, cols], out_ref.at[:, cols], st_sem.at[n])
        c.start()
        stores.append(c)

    finish(GROUP - 1, d)
    for n, o in enumerate(OFFSETS):
        o_copies[n].wait_recv()
        finish(n, source(o))
    for c in f_copies + m_copies + h_copies + list(r_copies.values()) + o_copies:
        c.wait_send()
    for c in stores:
        c.wait()


def on_device(query_gate, key_gate, value_in, filters, skip_gain):
    width = GROUP * LANES
    hops = (NZ - 1) * PIECES
    arrays = [jnp.asarray(t) for t in tables()]
    vm = pltpu.VMEM
    dma = pltpu.SemaphoreType.DMA
    return pl.pallas_call(
        kernel,
        name="hyena",
        out_shape=jax.ShapeDtypeStruct((ROWS, width), F32),
        in_specs=[pl.BlockSpec(memory_space=pl.ANY)] * 9,
        out_specs=pl.BlockSpec(memory_space=pl.ANY),
        scratch_shapes=[
            vm((ROWS, width), F32),
            vm((ROWS, width), F32),
            vm((ROWS, width), F32),
            vm((LAGS, width), F32),
            vm((1, width), F32),
            vm((SPEC, ROWS), BF16),
            vm((SPEC, ROWS), BF16),
            vm((ROWS, SPEC), BF16),
            vm((ROWS, SPEC), BF16),
            vm((GROUP, ROWS, LANES), F32),
            vm((2 * GROUP, ROWS, LANES), F32),
            vm((NZ, ROWS, LANES), F32),
            vm((2 * GROUP, SPEC, LANES), F32),
            vm((NZ, SPEC, LANES), F32),
            vm((2 * GROUP - 1, SPEC, LANES), F32),
            vm((SPEC, LANES), F32),
            vm((GROUP - 1, ROWS, LANES), F32),
            vm((GROUP, ROWS, LANES), F32),
            vm((ROWS, width), F32),
            dma((9,)),
            dma((GROUP - 1,)), dma((GROUP - 1,)),
            dma((GROUP - 1,)), dma((GROUP - 1,)),
            dma((GROUP,)), dma((GROUP,)),
            dma((hops,)), dma((hops,)),
            dma((GROUP - 1,)), dma((GROUP - 1,)),
            dma((GROUP,)),
        ],
        compiler_params=pltpu.CompilerParams(
            collective_id=0, has_side_effects=True, vmem_limit_bytes=48 << 20
        ),
    )(key_gate, value_in, query_gate, filters, skip_gain.reshape(1, width), *arrays)


def solution(mesh):
    in_specs = (P("seq", "ch"), P("seq", "ch"), P("seq", "ch"), P("seq", "ch"), P("ch"))
    return jax.shard_map(
        on_device, mesh=mesh, in_specs=in_specs, out_specs=P("seq", "ch"), check_vma=False
    )
```

time: 549 us -> 67.3 us (0.12)
  the two profiles are of different devices: /device:TPU:128 before, /device:TPU:2 now
where the time goes in v1:
time: 67.3 us; the launch traced here: 67 us
  Pallas kernels  56.9 us (85%)
  local copies, waits for them, and re-layouts  10 us (15%)
    pallas_call x1, Pallas kernels, on_device(): pl.pallas_call(kernel, name='hyena', out_shape=jax.ShapeDtypeStruct((ROWS...  56.9 us
    unnamed x19, local copies, waits for them, and re-layouts  10 us

profile of v1, /device:TPU:2, one launch (start us, length us, event | category | flops | bytes accessed | tf_op | source)
XLA Modules:
  0.0 67.0 jit_solution(7230088790228652834)
XLA Ops:
  0.0 0.0 copy-start
  0.0 1.2 %copy-done = f32[256,1024]{1,0:T(8,128)S(1)} copy-done((f32[256,1024]{1,0:T(8,128)S(1)}, f32[256,1024]{1,0:T(8,128)}, u32[]{:S(2)}) %copy-start) | copy-done | bytes 1048600
  1.2 0.0 copy-start.1
  1.2 1.2 %copy-done.1 = f32[256,1024]{1,0:T(8,128)S(1)} copy-done((f32[256,1024]{1,0:T(8,128)S(1)}, f32[256,1024]{1,0:T(8,128)}, u32[]{:S(2)}) %copy-start.1) | copy-done | bytes 1048600
  2.5 0.0 copy-start.2
  2.5 1.2 %copy-done.2 = f32[256,1024]{1,0:T(8,128)S(1)} copy-done((f32[256,1024]{1,0:T(8,128)S(1)}, f32[256,1024]{1,0:T(8,128)}, u32[]{:S(2)}) %copy-start.2) | copy-done | bytes 1048600
  3.7 0.0 copy-start.3
  3.7 0.9 %copy-done.3 = bf16[256,512]{1,0:T(8,128)(2,1)S(1)} copy-done((bf16[256,512]{1,0:T(8,128)(2,1)S(1)}, bf16[256,512]{1,0:T(8,128)(2,1)}, u32[]{:S(2)}) %copy-start.3) | copy-done | bytes 262168
  4.6 0.0 copy-start.4
  4.6 0.9 %copy-done.4 = bf16[256,512]{1,0:T(8,128)(2,1)S(1)} copy-done((bf16[256,512]{1,0:T(8,128)(2,1)S(1)}, bf16[256,512]{1,0:T(8,128)(2,1)}, u32[]{:S(2)}) %copy-start.4) | copy-done | bytes 262168
  5.6 0.0 copy-start.5
  5.6 0.9 %copy-done.5 = bf16[512,256]{1,0:T(8,128)(2,1)S(1)} copy-done((bf16[512,256]{1,0:T(8,128)(2,1)S(1)}, bf16[512,256]{1,0:T(8,128)(2,1)}, u32[]{:S(2)}) %copy-start.5) | copy-done | bytes 262168
  6.5 0.0 copy-start.6
  6.5 0.9 %copy-done.6 = bf16[512,256]{1,0:T(8,128)(2,1)S(1)} copy-done((bf16[512,256]{1,0:T(8,128)(2,1)S(1)}, bf16[512,256]{1,0:T(8,128)(2,1)}, u32[]{:S(2)}) %copy-start.6) | copy-done | bytes 262168
  7.5 0.0 copy-start.7
  7.5 0.9 %copy-done.7 = f32[32,1024]{1,0:T(8,128)S(1)} copy-done((f32[32,1024]{1,0:T(8,128)S(1)}, f32[32,1024]{1,0:T(8,128)}, u32[]{:S(2)}) %copy-start.7) | copy-done | bytes 131096
  8.4 0.0 copy-start.8
  8.4 0.7 %copy-done.8 = f32[1024]{0:T(1024)S(1)} copy-done((f32[1024]{0:T(1024)S(1)}, f32[1024]{0:T(1024)}, u32[]{:S(2)}) %copy-start.8) | copy-done | bytes 4120
  9.1 56.9 %hyena.1 = f32[256,1024]{1,0:T(8,128)S(1)} custom-call(f32[256,1024]{1,0:T(8,128)S(1)} %copy-done, f32[256,1024]{1,0:T(8,128)S(1)} %copy-done.1, f32[256,1024]{1,0:T(8,128)S(1)} %copy-done.2, f32[32,1024]{1,0:T(8,128)S(1)} %copy-done.7, f32[1,1024]{1,0:T(1,128)S(1)} %bitcast.1, bf16[512,256]{1,0:T(8,128)(2,1)S(1)} %copy-done.6, ...), custom_call_target="tpu_custom_call" | custom-call | tf_op jit(solution)/shard_map/hyena/pallas_call | solution.py:254
  66.0 1.0 %copy.11 = f32[256,1024]{1,0:T(8,128)} copy(f32[256,1024]{1,0:T(8,128)S(1)} %hyena.1) | data formatting | bytes 2097152
Async XLA Ops:
  0.0 1.2 %copy-start = (f32[256,1024]{1,0:T(8,128)S(1)}, f32[256,1024]{1,0:T(8,128)}, u32[]{:S(2)}) copy-start(f32[256,1024]{1,0:T(8,128)} %k_in.1) | copy-start | bytes 3145732
  1.2 1.2 %copy-start.1 = (f32[256,1024]{1,0:T(8,128)S(1)}, f32[256,1024]{1,0:T(8,128)}, u32[]{:S(2)}) copy-start(f32[256,1024]{1,0:T(8,128)} %v_in.1) | copy-start | bytes 3145732
  2.5 1.2 %copy-start.2 = (f32[256,1024]{1,0:T(8,128)S(1)}, f32[256,1024]{1,0:T(8,128)}, u32[]{:S(2)}) copy-start(f32[256,1024]{1,0:T(8,128)} %q_in.1) | copy-start | bytes 3145732
  3.7 0.9 %copy-start.3 = (bf16[256,512]{1,0:T(8,128)(2,1)S(1)}, bf16[256,512]{1,0:T(8,128)(2,1)}, u32[]{:S(2)}) copy-start(bf16[256,512]{1,0:T(8,128)(2,1)} %constant.11.clone.gl_in) | copy-start | bytes 786436
  4.6 0.9 %copy-start.4 = (bf16[256,512]{1,0:T(8,128)(2,1)S(1)}, bf16[256,512]{1,0:T(8,128)(2,1)}, u32[]{:S(2)}) copy-start(bf16[256,512]{1,0:T(8,128)(2,1)} %constant.10.clone.gh_in) | copy-start | bytes 786436
  5.6 0.9 %copy-start.5 = (bf16[512,256]{1,0:T(8,128)(2,1)S(1)}, bf16[512,256]{1,0:T(8,128)(2,1)}, u32[]{:S(2)}) copy-start(bf16[512,256]{1,0:T(8,128)(2,1)} %constant.9.clone.cl_in) | copy-start | bytes 786436
  6.5 0.9 %copy-start.6 = (bf16[512,256]{1,0:T(8,128)(2,1)S(1)}, bf16[512,256]{1,0:T(8,128)(2,1)}, u32[]{:S(2)}) copy-start(bf16[512,256]{1,0:T(8,128)(2,1)} %constant.8.clone.ch_in) | copy-start | bytes 786436
  7.5 0.9 %copy-start.7 = (f32[32,1024]{1,0:T(8,128)S(1)}, f32[32,1024]{1,0:T(8,128)}, u32[]{:S(2)}) copy-start(f32[32,1024]{1,0:T(8,128)} %f_in.1) | copy-start | bytes 393220
  8.4 0.7 %copy-start.8 = (f32[1024]{0:T(1024)S(1)}, f32[1024]{0:T(1024)}, u32[]{:S(2)}) copy-start(f32[1024]{0:T(1024)} %param.13) | copy-start | bytes 12292

commit v2 on v1

--- a/solution.py
+++ b/solution.py
@@ -286,7 +286,7 @@
             dma((GROUP,)),
         ],
         compiler_params=pltpu.CompilerParams(
-            collective_id=0, has_side_effects=True, vmem_limit_bytes=48 << 20
+            collective_id=0, has_side_effects=True, vmem_limit_bytes=61 << 20
         ),
     )(key_gate, value_in, query_gate, filters, skip_gain.reshape(1, width), *arrays)
 

time: 67.3 us -> 59.5 us (0.88)
  local copies, waits for them, and re-layouts: 10 us -> 2.31 us
    unnamed x19 -> x1, local copies, waits for them, and re-layouts: 10 us -> 2.31 us
where the time goes in v2:
time: 59.5 us; the launch traced here: 59.4 us
  Pallas kernels  57 us (96%)
  local copies, waits for them, and re-layouts  2.31 us (4%)
    pallas_call x1, Pallas kernels, on_device(): pl.pallas_call(kernel, name='hyena', out_shape=jax.ShapeDtypeStruct((ROWS...  57 us
    unnamed x1, local copies, waits for them, and re-layouts  2.31 us

profile of v2, /device:TPU:2, one launch (start us, length us, event | category | flops | bytes accessed | tf_op | source)
XLA Modules:
  0.0 59.4 jit_solution(9529211443196451126)
XLA Ops:
  0.0 57.0 %hyena.1 = f32[256,1024]{1,0:T(8,128)} custom-call(f32[256,1024]{1,0:T(8,128)} %k_in.1, f32[256,1024]{1,0:T(8,128)} %v_in.1, f32[256,1024]{1,0:T(8,128)} %q_in.1, f32[32,1024]{1,0:T(8,128)} %f_in.1, f32[1,1024]{1,0:T(1,128)} %bitcast.1, bf16[512,256]{1,0:T(8,128)(2,1)} %constant.8.clone.ch_in, bf16[512,256]{1,0:T(8,128)(2,1)} %constant.9.clone.cl_in, ...), custom_call_target="tpu_custom_call" | custom-call | tf_op jit(solution)/shard_map/hyena/pallas_call | solution.py:254
  57.0 2.3 %copy.11 = f32[256,1024]{1,0:T(8,128)} copy(f32[256,1024]{1,0:T(8,128)} %hyena.1) | data formatting | bytes 2097152

commit v3 on v2

--- a/solution.py
+++ b/solution.py
@@ -17,7 +17,7 @@
 GROUP = NX * NY
 LAGS = ROWS // GROUP
 SPEC = 2 * ROWS
-PIECES = 2
+PIECES = 4
 OFFSETS = [(0, 1), (0, 3), (1, 0), (1, 1), (1, 3), (0, 2), (1, 2)]
 
 
@@ -165,6 +165,17 @@
         block = (z + h + 1) % NZ
         forward(fb, block, fy, block)
 
+    def window(n, carry):
+        def tile(r, carry):
+            at = pl.ds(pl.multiple_of(r * 16, 16), 16)
+            im = pl.ds(pl.multiple_of(r * 16 + ROWS, 16), 16)
+            w[n, at] = y[n, at] + y[n + 1, im]
+            w[n, im] = y[n, im] - y[n + 1, at]
+            return carry
+
+        return lax.fori_loop(0, ROWS // 16, tile, carry, unroll=4)
+
+    lax.fori_loop(GROUP, 2 * GROUP - 1, window, 0)
     inside = (z > 0).astype(F32)
 
     def take(n, j):
@@ -186,17 +197,7 @@
     for n in range(4, GROUP - 1):
         take(n, source(OFFSETS[n]))
 
-    def window(n, carry):
-        def tile(r, carry):
-            at = pl.ds(pl.multiple_of(r * 16, 16), 16)
-            im = pl.ds(pl.multiple_of(r * 16 + ROWS, 16), 16)
-            w[n, at] = y[n, at] + y[n + 1, im]
-            w[n, im] = y[n, im] - y[n + 1, at]
-            return carry
-
-        return lax.fori_loop(0, ROWS // 16, tile, carry)
-
-    lax.fori_loop(0, 2 * GROUP - 1, window, 0)
+    lax.fori_loop(0, GROUP, window, 0)
 
     def output(i):
         def tile(r, carry):

time: 59.5 us -> 56.1 us (0.943)
  Pallas kernels: 57 us -> 53.3 us
    pallas_call x1, Pallas kernels: 57 us -> 53.3 us  [on_device(): pl.pallas_call(kernel, name='hyena', out_shape=jax.ShapeDtypeStruct((ROWS...]
where the time goes in v3:
time: 56.1 us; the launch traced here: 55.6 us
  Pallas kernels  53.3 us (95%)
  local copies, waits for them, and re-layouts  2.31 us (4%)
    pallas_call x1, Pallas kernels, on_device(): pl.pallas_call(kernel, name='hyena', out_shape=jax.ShapeDtypeStruct((ROWS...  53.3 us
    unnamed x1, local copies, waits for them, and re-layouts  2.31 us

profile of v3, /device:TPU:2, one launch (start us, length us, event | category | flops | bytes accessed | tf_op | source)
XLA Modules:
  0.0 55.6 jit_solution(17049863419604510727)
XLA Ops:
  0.0 53.3 %hyena.1 = f32[256,1024]{1,0:T(8,128)} custom-call(f32[256,1024]{1,0:T(8,128)} %k_in.1, f32[256,1024]{1,0:T(8,128)} %v_in.1, f32[256,1024]{1,0:T(8,128)} %q_in.1, f32[32,1024]{1,0:T(8,128)} %f_in.1, f32[1,1024]{1,0:T(1,128)} %bitcast.1, bf16[512,256]{1,0:T(8,128)(2,1)} %constant.8.clone.ch_in, bf16[512,256]{1,0:T(8,128)(2,1)} %constant.9.clone.cl_in, ...), custom_call_target="tpu_custom_call" | custom-call | tf_op jit(solution)/shard_map/hyena/pallas_call | solution.py:255
  53.3 2.3 %copy.11 = f32[256,1024]{1,0:T(8,128)} copy(f32[256,1024]{1,0:T(8,128)} %hyena.1) | data formatting | bytes 2097152
